TPU v7x, 256 devices: a whole 4x4x8 slice. The times are simulated.
256 devices in a mesh: row: 16 (over y, z_hi), col: 16 (over z_lo, x, core).
Axes of the slice: x: 4, y: 4, z: 8 (z_hi: 4, z_lo: 2; z = z_hi * 2 + z_lo), core: 2. Of those that a mesh axis runs over, the one named last changes fastest.
Arguments:
- pair: bfloat16 [2048, 2048, 128], P('row', 'col'), may hold values from -6 to 6
- pair_mask: int32 [2048, 2048], P('row', 'col'), may hold values 0 or 1
- in_gain: float32 [2, 128], replicated, may hold values from 0.1 to 1.9
- in_bias: float32 [2, 128], replicated, may hold values from -2 to 2
- proj_weight: bfloat16 [2, 128, 512], replicated, may hold values from -0.5 to 0.5
- gate_weight: bfloat16 [2, 128, 128], replicated, may hold values from -0.5 to 0.5
- out_gain: float32 [2, 128], replicated, may hold values from 0.1 to 1.9
- out_bias: float32 [2, 128], replicated, may hold values from -2 to 2
- out_weight: bfloat16 [2, 128, 128], replicated, may hold values from -0.5 to 0.5
Outputs:
- updated: bfloat16 [2048, 2048, 128], P('row', 'col')
All inputs are finite; a program needn't handle non-finite values. No bound on the sum of `pair_mask` on one device may be relied on, other than what follows from the above.
Results may differ from a plain program's by a relative error of at most 0.015.
Values may be sent and summed in bfloat16 or wider, within the bound.
A program may use at most 128 MiB of HBM per device.

v0:
```python
import jax
import jax.numpy as jnp
from jax import lax
from jax.sharding import PartitionSpec as P

WIN_DEV = 8


epsilon = 1e-05


def from_root(value, axis, source):
    kept = jnp.where(lax.axis_index(axis) == source, value, 0).astype(value.dtype)
    return lax.psum(kept, axis)


def normalize(values, gain, bias_in):
    centre = jnp.mean(values, -1, keepdims=True)
    shifted = values - centre
    variance = jnp.mean(shifted * shifted, -1, keepdims=True)
    return shifted * lax.rsqrt(variance + epsilon) * gain + bias_in


def project(normed, window_mask, weight):
    channels = weight.shape[0]
    leading = normed.shape[:-1]
    projected = jnp.dot(normed.reshape(-1, channels), weight, preferred_element_type=jnp.float32)
    projected = projected.reshape(leading + (4 * channels,))
    keep_mask = window_mask.astype(jnp.float32)[..., None]
    first = (
        keep_mask
        * jax.nn.sigmoid(projected[..., :channels])
        * projected[..., channels : 2 * channels]
    )
    second = (
        keep_mask
        * jax.nn.sigmoid(projected[..., 2 * channels : 3 * channels])
        * projected[..., 3 * channels :]
    )
    return (first.astype(jnp.bfloat16), second.astype(jnp.bfloat16))


def finish(pair_block, normed, summed, gate_w, gain_out, bias_out, out_w):
    channels = gate_w.shape[0]
    gating = jax.nn.sigmoid(
        jnp.dot(normed.reshape(-1, channels), gate_w, preferred_element_type=jnp.float32)
    )
    scaled = normalize(summed, gain_out, bias_out).astype(jnp.bfloat16)
    update = jnp.dot(scaled.reshape(-1, channels), out_w, preferred_element_type=jnp.float32)
    wide = pair_block.astype(jnp.float32).reshape(-1, channels)
    return (wide + gating * update).reshape(pair_block.shape).astype(jnp.bfloat16)


def per_device(
    pair, pair_mask, in_gain, in_bias, proj_weight, gate_weight, out_gain, out_bias, out_weight
):
    per_col = lax.axis_size("row") // lax.axis_size("col")
    row_index = lax.axis_index("row")
    col_index = lax.axis_index("col")
    normed = normalize(pair.astype(jnp.float32), in_gain[0], in_bias[0]).astype(jnp.bfloat16)
    left_own, right_own = project(normed[:, :WIN_DEV], pair_mask[:, :WIN_DEV], proj_weight[0])
    left_side, mirrored = (
        lax.all_gather(left_own, "col", axis=1, tiled=True),
        lax.all_gather(right_own, "col", axis=1, tiled=True),
    )
    pieces = from_root(mirrored, "row", col_index * per_col + 0)
    right_side = pieces
    summed = jnp.einsum("ikc,jkc->ijc", left_side, right_side, preferred_element_type=jnp.float32)
    middle = finish(pair, normed, summed, gate_weight[0], out_gain[0], out_bias[0], out_weight[0])
    normed = normalize(middle.astype(jnp.float32), in_gain[1], in_bias[1]).astype(jnp.bfloat16)
    left_own, right_own = project(normed[:WIN_DEV], pair_mask[:WIN_DEV], proj_weight[1])
    gathered, right_side = (
        lax.all_gather(left_own, "row", axis=0, tiled=True),
        lax.all_gather(right_own, "row", axis=0, tiled=True),
    )
    left_side = from_root(gathered, "col", row_index // per_col)
    summed = jnp.einsum("kic,kjc->ijc", left_side, right_side, preferred_element_type=jnp.float32)
    return finish(middle, normed, summed, gate_weight[1], out_gain[1], out_bias[1], out_weight[1])


def solution(mesh):
    placed = (P("row", "col", None), P("row", "col"), P(), P(), P(), P(), P(), P(), P())
    return jax.shard_map(
        per_device, mesh=mesh, in_specs=placed, out_specs=P("row", "col", None), check_vma=False
    )
```

profile of v0, /device:TPU:1, one launch (start us, length us, event | category | flops | bytes accessed | tf_op | source)
XLA Modules:
  0.0 702.1 jit_solution(9774752980750353333)
XLA Ops:
  6.5 0.0 all-gather.5.cloned.1.call-start
  6.6 5.7 convert_reduce_fusion
  12.3 6.2 multiply_reduce_fusion.3
  18.5 0.0 copy-done.4
  18.6 0.0 copy-done.7
  18.6 0.0 copy-done.6
  18.6 7.5 %add_convert_fusion.4 = bf16[128,128,128]{2,0,1:T(8,128)(2,1)S(1)} fusion(f32[128]{0:T(128)S(1)} %get-tuple-element.24, f32[128]{0:T(128)S(1)} %get-tuple-element.31, f32[128,128]{0,1:T(8,128)S(1)} %add_rsqrt_fusion.3, f32[128,128]{0,1:T(8,128)S(1)} %broadcast_multiply_fusion.3, bf16[128,128,128]{2,1,0:T(8,128)(2,1)} %param.9), kind=kLoop, calls=%fused_computation.26 | loop fusion | flops 12582912 | bytes 8520704 | tf_op jit(solution)/shard_map/convert_element_type | solution.py:60
  26.1 0.0 copy-start.2
  26.1 2.0 copy-done.2
  28.1 0.0 copy-done.3
  28.1 0.4 fusion.27
  28.5 1.1 fusion.16
  29.7 0.0 all-gather.5.cloned.1.call-update
  29.7 0.0 all-gather.7.cloned.1.call-start
  29.7 0.7 all-gather.7.cloned.1.call-update
  30.4 0.0 all-reduce.3.cloned.1.call-start
  30.5 43.6 %all-gather.5.cloned.1.call-done = bf16[128,128,128]{2,0,1:T(8,128)(2,1)} async-done(((bf16[128,8,128]{2,0,1:T(8,128)(2,1)}), bf16[128,128,128]{2,0,1:T(8,128)(2,1)}) %all-gather.5.cloned.1.call-update) | async-done | bytes 4194320 | tf_op jit(solution)/shard_map/all_gather | solution.py:64
  74.1 7.3 %copy.53 = bf16[128,128,128]{1,0,2:T(8,128)(2,1)} copy(bf16[128,128,128]{2,0,1:T(8,128)(2,1)} %all-gather.5.cloned.1.call-done) | data formatting | bytes 8388608 | tf_op jit(solution)/shard_map/all_gather | solution.py:64
  81.4 2.2 broadcast_select_fusion.1
  83.6 0.0 all-reduce.3.cloned.1.call-update
  83.6 0.5 all-gather.11.cloned.1.call-start
  84.1 0.0 copy-start.1
  84.2 5.0 copy.51
  89.2 0.0 copy-done.1
  89.2 2.4 copy_convert_fusion
  91.6 0.0 copy-start.8
  91.7 0.0 copy-start.9
  91.7 0.0 copy-start.10
  91.7 8.1 %copy.50 = f32[128,128,128]{2,1,0:T(8,128)} copy(f32[128,128,128]{2,0,1:T(8,128)S(1)} %copy_convert_fusion) | data formatting | bytes 16777216 | tf_op jit(solution)/shard_map/convert_element_type | solution.py:50
  99.8 0.0 copy-done.8
  99.8 0.0 copy-done.10
  99.8 5.8 fusion.10
  105.6 10.4 %all-gather.7.cloned.1.call-done = bf16[128,128,128]{2,0,1:T(8,128)(2,1)} async-done(((bf16[128,8,128]{2,0,1:T(8,128)(2,1)}), bf16[128,128,128]{2,0,1:T(8,128)(2,1)}) %all-gather.7.cloned.1.call-update) | async-done | bytes 4194320 | tf_op jit(solution)/shard_map/all_gather | solution.py:63
  115.9 6.7 copy.54
  122.7 208.1 %all-reduce.3.cloned.1.call-done = bf16[128,128,128]{1,0,2:T(8,128)(2,1)} async-done(((bf16[128,128,128]{1,0,2:T(8,128)(2,1)}), bf16[128,128,128]{1,0,2:T(8,128)(2,1)}) %all-reduce.3.cloned.1.call-update) | async-done | bytes 4194320 | tf_op jit(solution)/shard_map/psum | solution.py:14
  330.8 4.7 bitcast_reduce_fusion.1
  335.5 0.9 multiply_reduce_fusion.2
  336.4 0.0 copy-start.5
  336.4 3.1 add_convert_fusion.3
  339.5 7.3 %copy.55 = bf16[128,128,128]{2,1,0:T(8,128)(2,1)} copy(bf16[128,128,128]{0,1,2:T(8,128)(2,1)} %add_convert_fusion.3) | data formatting | bytes 8388608 | tf_op jit(solution)/shard_map/convert_element_type | solution.py:48
  346.8 9.6 %fusion.42 = (f32[16384]{0:T(1024)S(1)}, f32[16384,128]{1,0:T(8,128)S(1)}) fusion(f32[16384,128]{1,0:T(8,128)} %bitcast.72, f32[16384,128]{1,0:T(8,128)} %fusion.10, bf16[16384,128]{1,0:T(8,128)(2,1)} %bitcast.73, bf16[2,128,128]{2,1,0:T(8,128)(2,1)S(1)} %copy-done.5), kind=kOutput, calls=%fused_computation.86 | convolution fusion | flops 547340288 | bytes 29458432 | tf_op jit(solution)/shard_map/dot_general | solution.py:49
  356.4 4.9 multiply_reduce_fusion.1
  361.4 0.5 fusion.15
  361.9 0.3 fusion.41
  362.1 0.2 copy.62
  362.4 0.2 copy.63
  362.6 0.2 copy.64
  362.9 0.2 copy.65
  363.1 1.1 multiply_convert_fusion
  364.2 0.0 all-gather.11.cloned.1.call-update
  364.2 0.0 all-gather.9.cloned.1.call-start
  364.3 0.5 all-gather.9.cloned.1.call-update
  364.8 0.3 all-reduce.5.cloned.1.call-start
  365.1 86.0 %all-gather.11.cloned.1.call-done = bf16[128,128,128]{1,0,2:T(8,128)(2,1)} async-done(((bf16[8,128,128]{1,0,2:T(8,128)(2,1)}), bf16[128,128,128]{1,0,2:T(8,128)(2,1)}) %all-gather.11.cloned.1.call-update) | async-done | bytes 4194320 | tf_op jit(solution)/shard_map/all_gather | solution.py:73
  451.0 2.3 broadcast_select_fusion
  453.3 0.0 all-reduce.5.cloned.1.call-update
  453.3 12.5 %fusion.9 = f32[16384,128]{1,0:T(8,128)} fusion(f32[16384,128]{1,0:T(8,128)} %copy-done, f32[128]{0:T(128)S(1)} %get-tuple-element.23, f32[128]{0:T(128)S(1)} %get-tuple-element.32, f32[16384]{0:T(1024)S(1)} %get-tuple-element.14, f32[16384]{0:T(1024)S(1)} %get-tuple-element.12, bf16[2,128,128]{2,1,0:T(8,128)(2,1)S(1)} %copy-done.10), kind=kOutput, calls=%fused_computation.13 | convolution fusion | flops 553648128 | bytes 16942080 | tf_op jit(solution)/shard_map/dot_general | solution.py:46
  465.9 68.6 %all-gather.9.cloned.1.call-done = bf16[128,128,128]{1,0,2:T(8,128)(2,1)} async-done(((bf16[8,128,128]{1,0,2:T(8,128)(2,1)}), bf16[128,128,128]{1,0,2:T(8,128)(2,1)}) %all-gather.9.cloned.1.call-update) | async-done | bytes 4194320 | tf_op jit(solution)/shard_map/all_gather | solution.py:74
  534.4 134.1 %all-reduce.5.cloned.1.call-done = bf16[128,128,128]{1,0,2:T(8,128)(2,1)} async-done(((bf16[128,128,128]{1,0,2:T(8,128)(2,1)}), bf16[128,128,128]{1,0,2:T(8,128)(2,1)}) %all-reduce.5.cloned.1.call-update) | async-done | bytes 4194320 | tf_op jit(solution)/shard_map/psum | solution.py:14
  668.5 5.0 bitcast_reduce_fusion
  673.5 0.9 multiply_reduce_fusion
  674.4 3.1 add_convert_fusion
  677.5 7.3 %copy.60 = bf16[128,128,128]{2,1,0:T(8,128)(2,1)} copy(bf16[128,128,128]{0,1,2:T(8,128)(2,1)} %add_convert_fusion) | data formatting | bytes 8388608 | tf_op jit(solution)/shard_map/convert_element_type | solution.py:48
  684.8 10.2 %fusion.7 = bf16[16384,128]{1,0:T(8,128)(2,1)} fusion(f32[16384,128]{1,0:T(8,128)} %copy-done, f32[16384,128]{1,0:T(8,128)} %fusion.9, bf16[16384,128]{1,0:T(8,128)(2,1)} %bitcast.74, bf16[2,128,128]{2,1,0:T(8,128)(2,1)S(1)} %copy-done.5), kind=kOutput, calls=%fused_computation.11 | convolution fusion | flops 543162368 | bytes 25198592 | tf_op jit(solution)/shard_map/dot_general | solution.py:49
  (21 shorter events, 0.2 us)
Async XLA Ops:
  6.5 12.0 %copy-start.4 = (s32[128,128]{1,0:T(8,128)S(1)}, s32[128,128]{1,0:T(8,128)}, u32[]{:S(2)}) copy-start(s32[128,128]{1,0:T(8,128)} %param.10) | copy-start | bytes 196612
  6.5 12.1 %copy-start.7 = (f32[2,128]{1,0:T(2,128)S(1)}, f32[2,128]{1,0:T(2,128)}, u32[]{:S(2)}) copy-start(f32[2,128]{1,0:T(2,128)} %param.11) | copy-start | bytes 3076
  6.5 12.1 %copy-start.6 = (f32[2,128]{1,0:T(2,128)S(1)}, f32[2,128]{1,0:T(2,128)}, u32[]{:S(2)}) copy-start(f32[2,128]{1,0:T(2,128)} %param.12) | copy-start | bytes 3076
  6.5 21.6 %copy-start.3 = (bf16[2,128,512]{2,1,0:T(8,128)(2,1)S(1)}, bf16[2,128,512]{2,1,0:T(8,128)(2,1)}, u32[]{:S(2)}) copy-start(bf16[2,128,512]{2,1,0:T(8,128)(2,1)} %param.13) | copy-start | bytes 786436
  6.5 67.5 %all-gather.5.cloned.1.call-start = ((), (), s32[]{:S(2)}) async-start(), calls=%async_computation | async-start | bytes 4456448 | tf_op jit(solution)/shard_map/all_gather | solution.py:64
  26.1 2.0 copy-start.2
  29.7 86.2 %all-gather.7.cloned.1.call-start = ((), (), s32[]{:S(2)}) async-start(), calls=%async_computation.2 | async-start | bytes 4456448 | tf_op jit(solution)/shard_map/all_gather | solution.py:63
  30.4 300.4 %all-reduce.3.cloned.1.call-start = ((), (), s32[]{:S(2)}) async-start(), calls=%async_computation.1 | async-start | bytes 8388608 | tf_op jit(solution)/shard_map/psum | solution.py:14
  83.6 367.4 %all-gather.11.cloned.1.call-start = ((), (), s32[]{:S(2)}) async-start(), calls=%async_computation.4 | async-start | bytes 4456448 | tf_op jit(solution)/shard_map/all_gather | solution.py:73
  84.1 5.1 copy-start.1
  91.6 8.1 %copy-start.8 = (f32[2,128]{1,0:T(2,128)S(1)}, f32[2,128]{1,0:T(2,128)}, u32[]{:S(2)}) copy-start(f32[2,128]{1,0:T(2,128)} %param.16) | copy-start | bytes 3076
  91.7 8.1 %copy-start.9 = (f32[2,128]{1,0:T(2,128)S(1)}, f32[2,128]{1,0:T(2,128)}, u32[]{:S(2)}) copy-start(f32[2,128]{1,0:T(2,128)} %param.15) | copy-start | bytes 3076
  91.7 8.1 %copy-start.10 = (bf16[2,128,128]{2,1,0:T(8,128)(2,1)S(1)}, bf16[2,128,128]{2,1,0:T(8,128)(2,1)}, u32[]{:S(2)}) copy-start(bf16[2,128,128]{2,1,0:T(8,128)(2,1)} %param.14) | copy-start | bytes 196612
  336.4 10.4 %copy-start.5 = (bf16[2,128,128]{2,1,0:T(8,128)(2,1)S(1)}, bf16[2,128,128]{2,1,0:T(8,128)(2,1)}, u32[]{:S(2)}) copy-start(bf16[2,128,128]{2,1,0:T(8,128)(2,1)} %param.17) | copy-start | bytes 196612
  356.4 5.0 copy-start
  364.2 170.2 %all-gather.9.cloned.1.call-start = ((), (), s32[]{:S(2)}) async-start(), calls=%async_computation.3 | async-start | bytes 4456448 | tf_op jit(solution)/shard_map/all_gather | solution.py:74
  364.8 303.7 %all-reduce.5.cloned.1.call-start = ((), (), s32[]{:S(2)}) async-start(), calls=%async_computation.5 | async-start | bytes 8388608 | tf_op jit(solution)/shard_map/psum | solution.py:14
Sparse Core Ops, SparseCore 0:
  29.8 44.2 all-gather.4
  75.9 39.9 all-gather.6
  118.6 212.1 all-reduce.2
  364.3 86.6 all-gather.10
  453.3 81.1 all-gather.8
  537.0 131.5 all-reduce.4
where the time goes:
time: 709 us; the launch traced here: 702 us
  waiting for transfers between devices  552 us (78%)
  matrix products  48.7 us (7%)
  local copies, waits for them, and re-layouts  45 us (6%)
  other arithmetic  41.5 us (6%)
  between operations  14 us (2%)
    psum x2, waiting for transfers between devices, from_root(): return lax.psum(kept, axis)  342 us
    all_gather x1, waiting for transfers between devices, per_device(): lax.all_gather(left_own, 'row', axis=0, tiled=True)  86 us
    all_gather x1, waiting for transfers between devices, per_device(): lax.all_gather(right_own, 'row', axis=0, tiled=True)  68.6 us
    all_gather x1, waiting for transfers between devices, per_device(): lax.all_gather(right_own, 'col', axis=1, tiled=True)  43.6 us
    dot_general x2, matrix products, finish(): jnp.dot(scaled.reshape(-1, channels), out_w, preferred_element_type=jnp.f...  19.8 us
    dot_general x2, matrix products, finish(): jnp.dot(normed.reshape(-1, channels), gate_w, preferred_element_type=jnp....  18.3 us
    convert_element_type x2, local copies, waits for them, and re-layouts, finish(): scaled = normalize(summed, gain_out, bias_out).astype(jnp.bfloat16)  14.5 us
  transfers between devices with their start and end apart: 6, of which 6 were waited for; matrix products, arithmetic and copies ran while one was open for 7% of the time, Pallas kernels for 0%

commit v1 on v0

--- a/solution.py
+++ b/solution.py
@@ -9,9 +9,10 @@
 epsilon = 1e-05
 
 
-def from_root(value, axis, source):
-    kept = jnp.where(lax.axis_index(axis) == source, value, 0).astype(value.dtype)
-    return lax.psum(kept, axis)
+def swap_axes(value):
+    size = lax.axis_size("row")
+    pairs = [(r * size + c, c * size + r) for r in range(size) for c in range(size)]
+    return lax.ppermute(value, ("row", "col"), pairs)
 
 
 def normalize(values, gain, bias_in):
@@ -54,26 +55,18 @@
 def per_device(
     pair, pair_mask, in_gain, in_bias, proj_weight, gate_weight, out_gain, out_bias, out_weight
 ):
-    per_col = lax.axis_size("row") // lax.axis_size("col")
-    row_index = lax.axis_index("row")
-    col_index = lax.axis_index("col")
     normed = normalize(pair.astype(jnp.float32), in_gain[0], in_bias[0]).astype(jnp.bfloat16)
     left_own, right_own = project(normed[:, :WIN_DEV], pair_mask[:, :WIN_DEV], proj_weight[0])
-    left_side, mirrored = (
-        lax.all_gather(left_own, "col", axis=1, tiled=True),
-        lax.all_gather(right_own, "col", axis=1, tiled=True),
-    )
-    pieces = from_root(mirrored, "row", col_index * per_col + 0)
-    right_side = pieces
+    swapped = swap_axes(right_own)
+    left_side = lax.all_gather(left_own, "col", axis=1, tiled=True)
+    right_side = lax.all_gather(swapped, "row", axis=1, tiled=True)
     summed = jnp.einsum("ikc,jkc->ijc", left_side, right_side, preferred_element_type=jnp.float32)
     middle = finish(pair, normed, summed, gate_weight[0], out_gain[0], out_bias[0], out_weight[0])
     normed = normalize(middle.astype(jnp.float32), in_gain[1], in_bias[1]).astype(jnp.bfloat16)
     left_own, right_own = project(normed[:WIN_DEV], pair_mask[:WIN_DEV], proj_weight[1])
-    gathered, right_side = (
-        lax.all_gather(left_own, "row", axis=0, tiled=True),
-        lax.all_gather(right_own, "row", axis=0, tiled=True),
-    )
-    left_side = from_root(gathered, "col", row_index // per_col)
+    swapped = swap_axes(left_own)
+    right_side = lax.all_gather(right_own, "row", axis=0, tiled=True)
+    left_side = lax.all_gather(swapped, "col", axis=0, tiled=True)
     summed = jnp.einsum("kic,kjc->ijc", left_side, right_side, preferred_element_type=jnp.float32)
     return finish(middle, normed, summed, gate_weight[1], out_gain[1], out_bias[1], out_weight[1])
 

time: 709 us -> 364 us (0.51)
  waiting for transfers between devices: 552 us -> 186 us
  starting transfers between devices: 0.91 us -> 14.5 us
  local copies, waits for them, and re-layouts: 45 us -> 58.1 us
    psum x2 -> x0, waiting for transfers between devices: 342 us -> none  [from_root(): return lax.psum(kept, axis)]
    all_gather x4, waiting for transfers between devices: 209 us -> 175 us  [the longest x1 70.7 us: per_device(): right_side = lax.all_gather(swapped, 'row', axis=1, tiled=True)]
    ppermute x0 -> x2, starting transfers between devices: none -> 13.9 us  [swap_axes(): return lax.ppermute(value, ('row', 'col'), pairs)]
    all_gather x2 -> x4, local copies, waits for them, and re-layouts: 14 us -> 26.9 us  [the longest x1 6.75 us: per_device(): left_side = lax.all_gather(swapped, 'col', axis=0, tiled=True)]
    ppermute x0 -> x2, waiting for transfers between devices: none -> 10.7 us  [swap_axes(): return lax.ppermute(value, ('row', 'col'), pairs)]
  transfers between devices with their start and end apart: 6 -> 6, of which waited for: 6 -> 6; matrix products, arithmetic and copies ran while one was open for 7% -> 13% of each run, Pallas kernels for 0% -> 0%
where the time goes in v1:
time: 364 us; the launch traced here: 358 us
  waiting for transfers between devices  186 us (51%)
  local copies, waits for them, and re-layouts  58.1 us (16%)
  matrix products  49.1 us (13%)
  other arithmetic  36.8 us (10%)
  starting transfers between devices  14.5 us (4%)
  between operations  13.6 us (4%)
    all_gather x1, waiting for transfers between devices, per_device(): right_side = lax.all_gather(swapped, 'row', axis=1, tiled=True)  70.7 us
    all_gather x1, waiting for transfers between devices, per_device(): right_side = lax.all_gather(right_own, 'row', axis=0, tiled=True)  53.7 us
    all_gather x1, waiting for transfers between devices, per_device(): left_side = lax.all_gather(swapped, 'col', axis=0, tiled=True)  36.5 us
    dot_general x2, matrix products, finish(): jnp.dot(scaled.reshape(-1, channels), out_w, preferred_element_type=jnp.f...  19.8 us
    dot_general x2, matrix products, finish(): jnp.dot(normed.reshape(-1, channels), gate_w, preferred_element_type=jnp....  18.3 us
    convert_element_type x2, local copies, waits for them, and re-layouts, finish(): scaled = normalize(summed, gain_out, bias_out).astype(jnp.bfloat16)  14.5 us
    all_gather x1, waiting for transfers between devices, per_device(): left_side = lax.all_gather(left_own, 'col', axis=1, tiled=True)  14.5 us
    ppermute x2, starting transfers between devices, swap_axes(): return lax.ppermute(value, ('row', 'col'), pairs)  13.9 us
  transfers between devices with their start and end apart: 6, of which 6 were waited for; matrix products, arithmetic and copies ran while one was open for 13% of the time, Pallas kernels for 0%

profile of v1, /device:TPU:1, one launch (start us, length us, event | category | flops | bytes accessed | tf_op | source)
XLA Modules:
  0.0 358.3 jit_solution(4211944232577037533)
XLA Ops:
  6.5 0.0 copy-start.6
  6.5 0.0 all-gather.7.cloned.1.call-start
  6.6 5.7 %convert_reduce_fusion = f32[128,128]{0,1:T(8,128)S(1)} fusion(bf16[128,128,128]{2,1,0:T(8,128)(2,1)} %param.9), kind=kLoop, calls=%fused_computation.28 | loop fusion | flops 4177920 | bytes 4259840 | tf_op jit(solution)/shard_map/reduce_sum | solution.py:19
  12.3 6.2 %multiply_reduce_fusion.3 = f32[128,128]{0,1:T(8,128)S(1)} fusion(f32[128,128]{0,1:T(8,128)S(1)} %broadcast_multiply_fusion.3, bf16[128,128,128]{2,1,0:T(8,128)(2,1)} %param.9), kind=kLoop, calls=%fused_computation.27 | loop fusion | flops 8372224 | bytes 4325376 | tf_op jit(solution)/shard_map/reduce_sum | solution.py:21
  18.5 0.0 copy-done.6
  18.6 0.0 copy-done.9
  18.6 0.0 copy-done.8
  18.6 7.5 %add_convert_fusion.4 = bf16[128,128,128]{2,0,1:T(8,128)(2,1)S(1)} fusion(f32[128]{0:T(128)S(1)} %get-tuple-element.20, f32[128]{0:T(128)S(1)} %get-tuple-element.27, f32[128,128]{0,1:T(8,128)S(1)} %add_rsqrt_fusion.3, f32[128,128]{0,1:T(8,128)S(1)} %broadcast_multiply_fusion.3, bf16[128,128,128]{2,1,0:T(8,128)(2,1)} %param.9), kind=kLoop, calls=%fused_computation.26 | loop fusion | flops 12582912 | bytes 8520704 | tf_op jit(solution)/shard_map/convert_element_type | solution.py:58
  26.1 0.0 copy-start.2
  26.1 2.0 copy-done.2
  28.1 0.0 copy-done.3
  28.1 0.4 fusion.37
  28.5 1.0 fusion.26
  29.6 0.0 all-gather.7.cloned.1.call-update
  29.6 0.0 all-gather.5.cloned.1.call-start
  29.7 6.3 %collective-permute-start = (bf16[128,8,128]{2,0,1:T(8,128)(2,1)S(1)}, bf16[128,8,128]{2,0,1:T(8,128)(2,1)S(1)}, u32[]{:S(2)}, u32[]{:S(2)}) collective-permute-start(bf16[128,8,128]{2,0,1:T(8,128)(2,1)S(1)} %get-tuple-element.8), channel_id=1, source_target_pairs={{0,0},{1,16},{2,32},{3,48},{4,64},{5,80},{6,96},{7,112},{8,128},{9... | collective-permute-start | bytes 786440 | tf_op jit(solution)/shard_map/ppermute | solution.py:15
  36.0 4.7 %collective-permute-done = bf16[128,8,128]{2,0,1:T(8,128)(2,1)S(1)} collective-permute-done((bf16[128,8,128]{2,0,1:T(8,128)(2,1)S(1)}, bf16[128,8,128]{2,0,1:T(8,128)(2,1)S(1)}, u32[]{:S(2)}, u32[]{:S(2)}) %collective-permute-start) | collective-permute-done | bytes 262176 | tf_op jit(solution)/shard_map/ppermute | solution.py:15
  40.7 0.7 copy-done.4
  41.4 0.0 all-gather.5.cloned.1.call-update
  41.4 0.5 all-gather.9.cloned.1.call-start
  41.9 0.0 copy-start.1
  41.9 5.0 %copy.39 = bf16[128,128,128]{2,1,0:T(8,128)(2,1)S(1)} copy(bf16[128,128,128]{2,0,1:T(8,128)(2,1)} %copy-done.2) | data formatting | bytes 8388608 | tf_op jit(solution)/shard_map/convert_element_type | solution.py:58
  47.0 0.0 copy-done.1
  47.0 2.4 copy_convert_fusion
  49.4 0.0 copy-start.10
  49.4 0.0 copy-start.11
  49.4 0.0 copy-start.12
  49.5 8.1 %copy.38 = f32[128,128,128]{2,1,0:T(8,128)} copy(f32[128,128,128]{2,0,1:T(8,128)S(1)} %copy_convert_fusion) | data formatting | bytes 16777216 | tf_op jit(solution)/shard_map/convert_element_type | solution.py:51
  57.5 0.0 copy-done.10
  57.5 0.0 copy-done.11
  57.5 0.0 copy-done.12
  57.6 5.8 %fusion.10 = f32[16384,128]{1,0:T(8,128)} fusion(bf16[16384,128]{1,0:T(8,128)(2,1)S(1)} %bitcast.75, bf16[2,128,128]{2,1,0:T(8,128)(2,1)S(1)} %copy-done.12), kind=kOutput, calls=%fused_computation.14 | convolution fusion | flops 543162368 | bytes 12615680 | tf_op jit(solution)/shard_map/dot_general | solution.py:47
  63.3 14.5 %all-gather.7.cloned.1.call-done = bf16[128,128,128]{2,0,1:T(8,128)(2,1)} async-done(((bf16[128,8,128]{2,0,1:T(8,128)(2,1)}), bf16[128,128,128]{2,0,1:T(8,128)(2,1)}) %all-gather.7.cloned.1.call-update) | async-done | bytes 4194320 | tf_op jit(solution)/shard_map/all_gather | solution.py:61
  77.9 6.7 %copy.42 = bf16[128,128,128]{0,1,2:T(8,128)(2,1)} copy(bf16[128,128,128]{2,0,1:T(8,128)(2,1)} %all-gather.7.cloned.1.call-done) | data formatting | bytes 8388608 | tf_op jit(solution)/shard_map/all_gather | solution.py:61
  84.6 70.7 %all-gather.5.cloned.1.call-done = bf16[128,128,128]{2,0,1:T(8,128)(2,1)} async-done(((bf16[128,8,128]{2,0,1:T(8,128)(2,1)}), bf16[128,128,128]{2,0,1:T(8,128)(2,1)}) %all-gather.5.cloned.1.call-update) | async-done | bytes 4194320 | tf_op jit(solution)/shard_map/all_gather | solution.py:62
  155.3 6.7 %copy.41 = bf16[128,128,128]{0,1,2:T(8,128)(2,1)} copy(bf16[128,128,128]{2,0,1:T(8,128)(2,1)} %all-gather.5.cloned.1.call-done) | data formatting | bytes 8388608 | tf_op jit(solution)/shard_map/all_gather | solution.py:62
  162.0 5.0 %bitcast_reduce_fusion.1 = (f32[128,128]{0,1:T(8,128)S(1)}, f32[128,128,128]{2,1,0:T(8,128)S(1)}) fusion(bf16[128,128,128]{0,1,2:T(8,128)(2,1)} %copy.41, bf16[128,128,128]{0,1,2:T(8,128)(2,1)} %copy.42), kind=kOutput, calls=%fused_computation.18 | convolution fusion | flops 538951680 | bytes 16842752 | tf_op jit(solution)/shard_map/ikc,jkc->ijc/dot_general | solution.py:63
  167.0 0.9 multiply_reduce_fusion.2
  167.9 0.0 copy-start.7
  167.9 3.1 add_convert_fusion.3
  171.0 7.3 %copy.43 = bf16[128,128,128]{2,1,0:T(8,128)(2,1)} copy(bf16[128,128,128]{0,1,2:T(8,128)(2,1)} %add_convert_fusion.3) | data formatting | bytes 8388608 | tf_op jit(solution)/shard_map/convert_element_type | solution.py:49
  178.3 0.0 copy-done.7
  178.3 9.6 %fusion.51 = (f32[16384]{0:T(1024)S(1)}, f32[16384,128]{1,0:T(8,128)S(1)}) fusion(f32[16384,128]{1,0:T(8,128)} %bitcast.72, f32[16384,128]{1,0:T(8,128)} %fusion.10, bf16[16384,128]{1,0:T(8,128)(2,1)} %bitcast.73, bf16[2,128,128]{2,1,0:T(8,128)(2,1)S(1)} %copy-done.7), kind=kOutput, calls=%fused_computation.95 | convolution fusion | flops 547340288 | bytes 29458432 | tf_op jit(solution)/shard_map/dot_general | solution.py:50
  187.9 0.0 copy-start
  187.9 4.9 %multiply_reduce_fusion.1 = f32[16384]{0:T(1024)S(1)} fusion(f32[16384,128]{1,0:T(8,128)S(1)} %get-tuple-element.24, f32[16384]{0:T(1024)S(1)} %get-tuple-element.10), kind=kLoop, calls=%fused_computation.23 | loop fusion | flops 6275072 | bytes 8519680 | tf_op jit(solution)/shard_map/reduce_sum | solution.py:21
  192.9 0.0 copy-done
  192.9 0.5 fusion.15
  193.4 1.0 fusion.16
  194.4 0.0 all-gather.9.cloned.1.call-update
  194.4 0.0 all-gather.11.cloned.1.call-start
  194.5 7.6 %collective-permute-start.1 = (bf16[8,128,128]{2,1,0:T(8,128)(2,1)S(1)}, bf16[8,128,128]{2,1,0:T(8,128)(2,1)S(1)}, u32[]{:S(2)}, u32[]{:S(2)}) collective-permute-start(bf16[8,128,128]{2,1,0:T(8,128)(2,1)S(1)} %get-tuple-element.5), channel_id=1, source_target_pairs={{0,0},{1,16},{2,32},{3,48},{4,64},{5,80},{6,96},{7,112},{8,128},{9... | collective-permute-start | bytes 786440 | tf_op jit(solution)/shard_map/ppermute | solution.py:15
  202.1 6.0 %collective-permute-done.1 = bf16[8,128,128]{2,1,0:T(8,128)(2,1)S(1)} collective-permute-done((bf16[8,128,128]{2,1,0:T(8,128)(2,1)S(1)}, bf16[8,128,128]{2,1,0:T(8,128)(2,1)S(1)}, u32[]{:S(2)}, u32[]{:S(2)}) %collective-permute-start.1) | collective-permute-done | bytes 262176 | tf_op jit(solution)/shard_map/ppermute | solution.py:15
  208.0 0.7 copy-done.5
  208.8 0.0 all-gather.11.cloned.1.call-update
  208.8 12.5 %fusion.9 = f32[16384,128]{1,0:T(8,128)} fusion(f32[16384,128]{1,0:T(8,128)} %copy-done, f32[128]{0:T(128)S(1)} %get-tuple-element.19, f32[128]{0:T(128)S(1)} %get-tuple-element.28, f32[16384]{0:T(1024)S(1)} %get-tuple-element.12, f32[16384]{0:T(1024)S(1)} %get-tuple-element.10, bf16[2,128,128]{2,1,0:T(8,128)(2,1)S(1)} %copy-done.12), kind=kOutput, calls=%fused_computation.13 | convolution fusion | flops 553648128 | bytes 16942080 | tf_op jit(solution)/shard_map/dot_general | solution.py:47
  221.3 53.7 %all-gather.9.cloned.1.call-done = bf16[128,128,128]{2,1,0:T(8,128)(2,1)} async-done(((bf16[8,128,128]{2,1,0:T(8,128)(2,1)}), bf16[128,128,128]{2,1,0:T(8,128)(2,1)}) %all-gather.9.cloned.1.call-update) | async-done | bytes 4194320 | tf_op jit(solution)/shard_map/all_gather | solution.py:68
  275.1 6.7 %copy.44 = bf16[128,128,128]{1,0,2:T(8,128)(2,1)} copy(bf16[128,128,128]{2,1,0:T(8,128)(2,1)} %all-gather.9.cloned.1.call-done) | data formatting | bytes 8388608 | tf_op jit(solution)/shard_map/all_gather | solution.py:68
  281.8 36.5 %all-gather.11.cloned.1.call-done = bf16[128,128,128]{2,1,0:T(8,128)(2,1)} async-done(((bf16[8,128,128]{2,1,0:T(8,128)(2,1)}), bf16[128,128,128]{2,1,0:T(8,128)(2,1)}) %all-gather.11.cloned.1.call-update) | async-done | bytes 4194320 | tf_op jit(solution)/shard_map/all_gather | solution.py:69
  318.3 6.7 %copy.45 = bf16[128,128,128]{1,0,2:T(8,128)(2,1)} copy(bf16[128,128,128]{2,1,0:T(8,128)(2,1)} %all-gather.11.cloned.1.call-done) | data formatting | bytes 8388608 | tf_op jit(solution)/shard_map/all_gather | solution.py:69
  325.0 5.0 %bitcast_reduce_fusion = (f32[128,128]{0,1:T(8,128)S(1)}, f32[128,128,128]{2,1,0:T(8,128)S(1)}) fusion(bf16[128,128,128]{1,0,2:T(8,128)(2,1)} %copy.44, bf16[128,128,128]{1,0,2:T(8,128)(2,1)} %copy.45), kind=kOutput, calls=%fused_computation.16 | convolution fusion | flops 538951680 | bytes 16842752 | tf_op jit(solution)/shard_map/kic,kjc->ijc/dot_general | solution.py:70
  330.1 0.9 multiply_reduce_fusion
  331.0 3.1 add_convert_fusion
  334.1 7.3 %copy.46 = bf16[128,128,128]{2,1,0:T(8,128)(2,1)} copy(bf16[128,128,128]{0,1,2:T(8,128)(2,1)} %add_convert_fusion) | data formatting | bytes 8388608 | tf_op jit(solution)/shard_map/convert_element_type | solution.py:49
  341.3 10.2 %fusion.7 = bf16[16384,128]{1,0:T(8,128)(2,1)} fusion(f32[16384,128]{1,0:T(8,128)} %copy-done, f32[16384,128]{1,0:T(8,128)} %fusion.9, bf16[16384,128]{1,0:T(8,128)(2,1)} %bitcast.74, bf16[2,128,128]{2,1,0:T(8,128)(2,1)S(1)} %copy-done.7), kind=kOutput, calls=%fused_computation.11 | convolution fusion | flops 543162368 | bytes 25198592 | tf_op jit(solution)/shard_map/dot_general | solution.py:50
  (18 shorter events, 0.2 us)
Async XLA Ops:
  6.5 12.0 %copy-start.6 = (s32[128,128]{1,0:T(8,128)S(1)}, s32[128,128]{1,0:T(8,128)}, u32[]{:S(2)}) copy-start(s32[128,128]{1,0:T(8,128)} %param.10) | copy-start | bytes 196612
  6.5 12.1 %copy-start.9 = (f32[2,128]{1,0:T(2,128)S(1)}, f32[2,128]{1,0:T(2,128)}, u32[]{:S(2)}) copy-start(f32[2,128]{1,0:T(2,128)} %param.11) | copy-start | bytes 3076
  6.5 12.1 %copy-start.8 = (f32[2,128]{1,0:T(2,128)S(1)}, f32[2,128]{1,0:T(2,128)}, u32[]{:S(2)}) copy-start(f32[2,128]{1,0:T(2,128)} %param.12) | copy-start | bytes 3076
  6.5 21.6 %copy-start.3 = (bf16[2,128,512]{2,1,0:T(8,128)(2,1)S(1)}, bf16[2,128,512]{2,1,0:T(8,128)(2,1)}, u32[]{:S(2)}) copy-start(bf16[2,128,512]{2,1,0:T(8,128)(2,1)} %param.13) | copy-start | bytes 786436
  6.5 71.3 %all-gather.7.cloned.1.call-start = ((), (), s32[]{:S(2)}) async-start(), calls=%async_computation.1 | async-start | bytes 4456448 | tf_op jit(solution)/shard_map/all_gather | solution.py:61
  26.1 2.0 copy-start.2
  29.6 125.6 %all-gather.5.cloned.1.call-start = ((), (), s32[]{:S(2)}) async-start(), calls=%async_computation | async-start | bytes 4456448 | tf_op jit(solution)/shard_map/all_gather | solution.py:62
  29.7 11.0 %collective-permute-start = (bf16[128,8,128]{2,0,1:T(8,128)(2,1)S(1)}, bf16[128,8,128]{2,0,1:T(8,128)(2,1)S(1)}, u32[]{:S(2)}, u32[]{:S(2)}) collective-permute-start(bf16[128,8,128]{2,0,1:T(8,128)(2,1)S(1)} %get-tuple-element.8), channel_id=1, source_target_pairs={{0,0},{1,16},{2,32},{3,48},{4,64},{5,80},{6,96},{7,112},{8,128},{9... | collective-permute-start | bytes 786440 | tf_op jit(solution)/shard_map/ppermute | solution.py:15
  40.7 0.7 copy-start.4
  41.4 233.7 %all-gather.9.cloned.1.call-start = ((), (), s32[]{:S(2)}) async-start(), calls=%async_computation.2 | async-start | bytes 4456448 | tf_op jit(solution)/shard_map/all_gather | solution.py:68
  41.9 5.1 %copy-start.1 = (bf16[128,128,128]{2,1,0:T(8,128)(2,1)S(1)}, bf16[128,128,128]{2,1,0:T(8,128)(2,1)}, u32[]{:S(2)}) copy-start(bf16[128,128,128]{2,1,0:T(8,128)(2,1)} %param.9) | copy-start | bytes 12582916
  49.4 8.1 %copy-start.10 = (f32[2,128]{1,0:T(2,128)S(1)}, f32[2,128]{1,0:T(2,128)}, u32[]{:S(2)}) copy-start(f32[2,128]{1,0:T(2,128)} %param.16) | copy-start | bytes 3076
  49.4 8.1 %copy-start.11 = (f32[2,128]{1,0:T(2,128)S(1)}, f32[2,128]{1,0:T(2,128)}, u32[]{:S(2)}) copy-start(f32[2,128]{1,0:T(2,128)} %param.15) | copy-start | bytes 3076
  49.4 8.1 %copy-start.12 = (bf16[2,128,128]{2,1,0:T(8,128)(2,1)S(1)}, bf16[2,128,128]{2,1,0:T(8,128)(2,1)}, u32[]{:S(2)}) copy-start(bf16[2,128,128]{2,1,0:T(8,128)(2,1)} %param.14) | copy-start | bytes 196612
  167.9 10.4 %copy-start.7 = (bf16[2,128,128]{2,1,0:T(8,128)(2,1)S(1)}, bf16[2,128,128]{2,1,0:T(8,128)(2,1)}, u32[]{:S(2)}) copy-start(bf16[2,128,128]{2,1,0:T(8,128)(2,1)} %param.17) | copy-start | bytes 196612
  187.9 5.0 %copy-start = (f32[16384,128]{1,0:T(8,128)}, f32[16384,128]{1,0:T(8,128)S(1)}, u32[]{:S(2)}) copy-start(f32[16384,128]{1,0:T(8,128)S(1)} %get-tuple-element.24) | copy-start | bytes 25165828
  194.4 123.9 %all-gather.11.cloned.1.call-start = ((), (), s32[]{:S(2)}) async-start(), calls=%async_computation.3 | async-start | bytes 4456448 | tf_op jit(solution)/shard_map/all_gather | solution.py:69
  194.5 13.6 %collective-permute-start.1 = (bf16[8,128,128]{2,1,0:T(8,128)(2,1)S(1)}, bf16[8,128,128]{2,1,0:T(8,128)(2,1)S(1)}, u32[]{:S(2)}, u32[]{:S(2)}) collective-permute-start(bf16[8,128,128]{2,1,0:T(8,128)(2,1)S(1)} %get-tuple-element.5), channel_id=1, source_target_pairs={{0,0},{1,16},{2,32},{3,48},{4,64},{5,80},{6,96},{7,112},{8,128},{9... | collective-permute-start | bytes 786440 | tf_op jit(solution)/shard_map/ppermute | solution.py:15
  208.0 0.7 copy-start.5
Sparse Core Ops, SparseCore 0:
  29.7 48.0 all-gather.6
  80.3 74.9 all-gather.4
  194.5 80.4 all-gather.8
  276.8 41.4 all-gather.10

commit v2 on v1

v2 whole, which is shorter than its diff:
```python
import functools

import jax
import jax.numpy as jnp
from jax import lax
from jax.experimental import pallas as pl
from jax.experimental.pallas import tpu as pltpu
from jax.sharding import PartitionSpec as P

C = 128
N = 128
WIN = 8
RING = 16
PIECE = C * WIN
HALF = PIECE // 2
EPS = 1e-5
MIB = 1024 * 1024
SEMS = 160
F32 = jnp.float32
BF16 = jnp.bfloat16


def xor(a, b):
    total = 0
    for bit in (1, 2, 4, 8):
        total = total + lax.rem(lax.div(a, bit) + lax.div(b, bit), 2) * bit
    return total


def sigmoid(z):
    return 0.5 * jnp.tanh(0.5 * z) + 0.5


def norm_lanes(x, gain, bias):
    centre = jnp.mean(x, -1, keepdims=True)
    s = x - centre
    var = jnp.mean(s * s, -1, keepdims=True)
    return s * lax.rsqrt(var + EPS) * gain + bias


def kernel(
    pair_ref, mask_ref, ing_ref, inb_ref, pw_ref, gw_ref, outg_ref, outb_ref, ow_ref, out_ref,
    wbuf, pairv, gate, a1, b1, a2, b2, xs, ha, hb, hat, hbt, own, mid_sw, parity, cols, maskt,
    ssem, rsem, lsem,
):
    r = lax.axis_index("row")
    c = lax.axis_index("col")
    y, zh = lax.div(r, 4), lax.rem(r, 4)
    zl, x, core = lax.div(c, 8), lax.rem(lax.div(c, 2), 4), lax.rem(c, 2)
    rc = xor(r, c)

    def row_at(dz, dy):
        return lax.rem(y + dy + 4, 4) * 4 + lax.rem(zh + dz + 4, 4)

    def col_at(dl, dx):
        return lax.rem(zl + dl, 2) * 8 + lax.rem(x + dx + 4, 4) * 2 + core

    sibling = c + 1 - 2 * core

    load_w = pltpu.make_async_copy(pair_ref.at[:, pl.ds(0, 16), :], wbuf, lsem.at[0])
    load_w.start()
    load_p = pltpu.make_async_copy(pair_ref, pairv, lsem.at[1])
    load_p.start()

    bar = pltpu.get_barrier_semaphore()

    def greet(dev):
        pl.semaphore_signal(bar, inc=1, device_id=dev, device_id_type=pl.DeviceIdType.MESH)

    fixed = [
        (row_at(0, 1), c), (row_at(0, -1), c), (row_at(1, 0), c), (row_at(-1, 0), c),
        (r, col_at(0, 1)), (r, col_at(0, -1)), (r, col_at(1, 0)), (r, sibling),
    ]
    for dev in fixed:
        greet(dev)

    @pl.when(c != 0)
    def _():
        greet((rc, c))

    @pl.when(r != 0)
    def _():
        greet((r, rc))

    copies = {}

    def make(name, src, dst, dev):
        n = len(copies)
        cp = pltpu.make_async_remote_copy(
            src_ref=src, dst_ref=dst, send_sem=ssem.at[n], recv_sem=rsem.at[n],
            device_id=dev, device_id_type=pl.DeviceIdType.MESH,
        )
        copies[name] = cp
        return cp

    def post(name, src, dst, dev):
        make(name, src, dst, dev).start()

    def got(name):
        copies[name].wait_recv()

    def half(ref, slot, h):
        return ref.at[slot, pl.ds(h * HALF, HALF), :]

    def prepare():
        row = lax.broadcasted_iota(jnp.int32, (256, N), 0)
        low = lax.rem(row, 16) < 8
        parity[0] = jnp.where(low, 1.0, 0.0).astype(BF16)
        parity[1] = jnp.where(low, 0.0, 1.0).astype(BF16)
        for d in range(2):
            cols[2 * d] = jnp.broadcast_to(outg_ref[pl.ds(d, 1), :], (C, C)).T
            cols[2 * d + 1] = jnp.broadcast_to(outb_ref[pl.ds(d, 1), :], (C, C)).T
        maskt[...] = mask_ref[...].astype(F32).T

    def project(n, d, store):
        h = jnp.dot(n, pw_ref[d], preferred_element_type=F32)
        store(ha, sigmoid(h[:, :C]) * h[:, C : 2 * C])
        store(hb, sigmoid(h[:, 2 * C : 3 * C]) * h[:, 3 * C :])

    def window_out():
        g, b = ing_ref[pl.ds(0, 1), :], inb_ref[pl.ds(0, 1), :]

        def body(t, carry):
            v = wbuf[pl.ds(t * 16, 16)].astype(F32)[:, :WIN, :].reshape(16 * WIN, C)
            n = norm_lanes(v, g, b).astype(BF16)

            def store(ref, val):
                ref[pl.ds(pl.multiple_of(t * 128, 128), 128), :] = val

            project(n, 0, store)
            return carry

        lax.fori_loop(0, 8, body, 0)
        for src, dst in ((ha, hat), (hb, hbt)):
            for k in range(WIN):
                t = src[pl.ds(k, N, stride=WIN), :].T
                dst[pl.ds(k, C, stride=WIN), :] = t * maskt[pl.ds(k, 1), :]

    def window_in():
        g, b = ing_ref[pl.ds(1, 1), :], inb_ref[pl.ds(1, 1), :]
        for k in range(WIN):
            v = pairv[k].astype(F32)
            n = norm_lanes(v, g, b).astype(BF16)
            m = mask_ref[pl.ds(k, 1), :].astype(F32)
            h = jnp.dot(n, pw_ref[1], preferred_element_type=F32)
            av = sigmoid(h[:, :C]) * h[:, C : 2 * C]
            bv = sigmoid(h[:, 2 * C : 3 * C]) * h[:, 3 * C :]
            hat[pl.ds(k, C, stride=WIN), :] = av.T * m
            hbt[pl.ds(k, C, stride=WIN), :] = bv.T * m

    def gate_rows(lo, hi, d):
        g, b = ing_ref[pl.ds(d, 1), :], inb_ref[pl.ds(d, 1), :]

        def body(t, carry):
            v = pairv[pl.ds(t * 2, 2)].astype(F32).reshape(2 * N, C)
            n = norm_lanes(v, g, b).astype(BF16)
            z = jnp.dot(n, gw_ref[d], preferred_element_type=F32)
            gate[pl.ds(t * 2, 2)] = sigmoid(z).astype(BF16).reshape(2, N, C)
            return carry

        lax.fori_loop(lo // 2, hi // 2, body, 0)

    def product(a, b, lo, hi):
        def body(t, carry):
            rows = pl.ds(pl.multiple_of(t * 16, 16), 16)
            lhs = a[:, rows, :].reshape(256, N)
            rhs = b[:, rows, :].reshape(256, N)
            both = jnp.concatenate([rhs * parity[0], rhs * parity[1]], axis=1)
            out = lax.dot_general(lhs, both, (((0,), (0,)), ((), ())), preferred_element_type=F32)
            base = pl.multiple_of(t * 16, 16)
            xs[:, pl.ds(base, 8), :] = out[:, :N].reshape(16, 8, N)
            xs[:, pl.ds(base + 8, 8), :] = out[:, N:].reshape(16, 8, N)
            return carry

        lax.fori_loop(lo, hi, body, 0)

    def finish(lo, hi, d):
        def body(t, carry):
            for i8 in range(8):
                v = xs[t, pl.ds(i8, C, stride=8), :]
                centre = jnp.mean(v, 0, keepdims=True)
                s = v - centre
                var = jnp.mean(s * s, 0, keepdims=True)
                n = s * lax.rsqrt(var + EPS) * cols[2 * d] + cols[2 * d + 1]
                u = lax.dot_general(
                    n.astype(BF16), ow_ref[d], (((0,), (0,)), ((), ())), preferred_element_type=F32
                )
                i = t * 8 + i8
                old = pairv[i].astype(F32)
                pairv[i] = (old + gate[i].astype(F32) * u).astype(BF16)
            return carry

        lax.fori_loop(lo, hi, body, 0)

    def gather_steps(p, a, b, lab_a, lab_b):
        steps = []

        def b_first(h):
            s = half(b, lab_b(r), h)
            for dz in (1, -1):
                post((p, "z", dz, h), s, s, (row_at(dz, 0), c))
            for dy in (1, -1):
                post((p, "y", 0, dy, h), s, s, (row_at(0, dy), c))

        def b_z(dz, h):
            got((p, "z", dz, h))
            s = half(b, lab_b(row_at(-dz, 0)), h)
            if (dz == 1) == (h == 0):
                post((p, "z", 2, h), s, s, (row_at(dz, 0), c))
            for dy in (1, -1):
                post((p, "y", -dz, dy, h), s, s, (row_at(0, dy), c))

        def b_z2(h):
            got((p, "z", 2, h))
            s = half(b, lab_b(row_at(2, 0)), h)
            for dy in (1, -1):
                post((p, "y", 2, dy, h), s, s, (row_at(0, dy), c))

        def b_y(q, dy, h):
            got((p, "y", q, dy, h))
            if (dy == 1) == (h == 0):
                s = half(b, lab_b(row_at(q, -dy)), h)
                post((p, "y2", q, h), s, s, (row_at(0, dy), c))

        def b_y2(q, h):
            got((p, "y2", q, h))

        def a_first(h):
            s = half(a, lab_a(c), h)
            post((p, "l", h), s, s, (r, col_at(1, 0)))
            for dx in (1, -1):
                post((p, "x", 0, dx, h), s, s, (r, col_at(0, dx)))
            post((p, "k", 0, 0, h), s, s, (r, sibling))

        def a_l(h):
            got((p, "l", h))
            s = half(a, lab_a(col_at(1, 0)), h)
            for dx in (1, -1):
                post((p, "x", 1, dx, h), s, s, (r, col_at(0, dx)))
            post((p, "k", 1, 0, h), s, s, (r, sibling))

        def a_x(q, dx, h):
            got((p, "x", q, dx, h))
            s = half(a, lab_a(col_at(q, -dx)), h)
            if (dx == 1) == (h == 0):
                post((p, "x2", q, h), s, s, (r, col_at(0, dx)))
            post((p, "k", q, -dx, h), s, s, (r, sibling))

        def a_x2(q, h):
            got((p, "x2", q, h))
            s = half(a, lab_a(col_at(q, 2)), h)
            post((p, "k", q, 2, h), s, s, (r, sibling))

        def a_k():
            for q in (0, 1):
                for dx in (0, 1, -1, 2):
                    for h in (0, 1):
                        got((p, "k", q, dx, h))

        f = functools.partial
        bs = [f(b_z, 1, 0), f(b_z, -1, 0), f(b_z, 1, 1), f(b_z, -1, 1), f(b_z2, 0), f(b_z2, 1)]
        for q in (0, 1, -1, 2):
            for h in (0, 1):
                bs += [f(b_y, q, 1, h), f(b_y, q, -1, h)]
        for q in (0, 1, -1, 2):
            bs += [f(b_y2, q, 0), f(b_y2, q, 1)]
        as_ = [f(a_l, 0), f(a_l, 1)]
        for q in (0, 1):
            for h in (0, 1):
                as_ += [f(a_x, q, 1, h), f(a_x, q, -1, h)]
        for q in (0, 1):
            as_ += [f(a_x2, q, 0), f(a_x2, q, 1)]
        as_ += [a_k]
        return b_first, bs, a_first, as_

    def weave(*lists):
        keyed = []
        for n, items in enumerate(lists):
            keyed += [((k + 0.5) / len(items), n, k, item) for k, item in enumerate(items)]
        return [e[3] for e in sorted(keyed, key=lambda e: e[:3])]

    def swap(name, src, dst, dev, moves):
        cp = make(name, src, dst, dev)

        @pl.when(moves)
        def _():
            cp.start()

        @pl.when(jnp.logical_not(moves))
        def _():
            keep = pltpu.make_async_copy(src, dst, lsem.at[2])
            keep.start()
            keep.wait()

    def swapped(name, moves):
        @pl.when(moves)
        def _():
            got(name)

    def part(ref, h):
        return ref.at[pl.ds(h * HALF, HALF), :]

    f = functools.partial

    prepare()
    load_w.wait()
    window_out()
    a1[c] = hat[...].astype(BF16)
    own[0] = hbt[...].astype(BF16)
    pl.semaphore_wait(bar, 8 + jnp.where(c != 0, 1, 0) + jnp.where(r != 0, 1, 0))
    for h in (0, 1):
        swap(("s1", h), part(own.at[0], h), part(mid_sw.at[0], h), (rc, c), c != 0)
    b_first, bs, a_first, as_ = gather_steps(0, a1, b1, lambda col: col, lambda row: xor(row, c))
    a_first(0)
    a_first(1)
    load_p.wait()

    def relay1(h):
        swapped(("s1", h), c != 0)
        swap(("s2", h), part(mid_sw.at[0], h), half(b1, c, h), (r, rc), r != 0)

    def begin1(h):
        swapped(("s2", h), r != 0)
        b_first(h)

    gates = [f(gate_rows, 8 * t, 8 * t + 8, 0) for t in range(16)]
    for step in weave([f(relay1, 0), f(relay1, 1)], gates[:3]):
        step()
    for step in weave([f(begin1, 0), f(begin1, 1)], as_[:4], gates[3:7]):
        step()
    for step in weave(bs, as_[4:], gates[7:]):
        step()

    product(a1, b1, 0, 64)
    finish(0, 1, 0)
    window_in()
    own[1] = hat[...].astype(BF16)
    b2[r] = hbt[...].astype(BF16)
    b_first, bs, a_first, as_ = gather_steps(1, a2, b2, lambda col: xor(r, col), lambda row: row)
    for h in (0, 1):
        swap(("t1", h), part(own.at[1], h), part(mid_sw.at[1], h), (r, rc), r != 0)
    b_first(0)
    b_first(1)

    def relay2(h):
        swapped(("t1", h), r != 0)
        swap(("t2", h), part(mid_sw.at[1], h), half(a2, r, h), (rc, c), c != 0)

    def begin2(h):
        swapped(("t2", h), c != 0)
        a_first(h)

    rest = []
    for t in range(1, 16):
        rest.append(f(finish, t, t + 1, 0))
    gates = [f(gate_rows, 8 * t, 8 * t + 8, 1) for t in range(16)]
    work = rest + gates
    for step in weave([f(relay2, 0), f(relay2, 1)], work[:4]):
        step()
    for step in weave([f(begin2, 0), f(begin2, 1)], bs[:2], work[4:8]):
        step()
    for step in weave(bs[2:], as_, work[8:]):
        step()

    product(a2, b2, 0, 64)
    outs = []
    for t in range(4):
        finish(4 * t, 4 * t + 4, 1)
        rows = pl.ds(32 * t, 32)
        cp = pltpu.make_async_copy(pairv.at[rows], out_ref.at[rows], lsem.at[3 + t])
        cp.start()
        outs.append(cp)
    guard = {"s1": c != 0, "s2": r != 0, "t1": r != 0, "t2": c != 0}
    for name, cp in copies.items():
        if name[0] in guard:
            pl.when(guard[name[0]])(cp.wait_send)
        else:
            cp.wait_send()
    for cp in outs:
        cp.wait()


def per_device(pair, mask, in_gain, in_bias, proj, gate_w, out_gain, out_bias, out_w):
    vm = pl.BlockSpec(memory_space=pltpu.VMEM)
    anyspace = pl.BlockSpec(memory_space=pl.ANY)
    cells = N * N * C
    return pl.pallas_call(
        kernel,
        out_shape=jax.ShapeDtypeStruct((N, N, C), BF16),
        in_specs=[anyspace] + [vm] * 8,
        out_specs=anyspace,
        scratch_shapes=[
            pltpu.VMEM((N, 16, C), BF16),
            pltpu.VMEM((N, N, C), BF16),
            pltpu.VMEM((N, N, C), BF16),
            pltpu.VMEM((RING, PIECE, N), BF16),
            pltpu.VMEM((RING, PIECE, N), BF16),
            pltpu.VMEM((RING, PIECE, N), BF16),
            pltpu.VMEM((RING, PIECE, N), BF16),
            pltpu.VMEM((16, 8 * C, N), F32),
            pltpu.VMEM((PIECE, C), F32),
            pltpu.VMEM((PIECE, C), F32),
            pltpu.VMEM((PIECE, N), F32),
            pltpu.VMEM((PIECE, N), F32),
            pltpu.VMEM((2, PIECE, N), BF16),
            pltpu.VMEM((2, PIECE, N), BF16),
            pltpu.VMEM((2, 256, N), BF16),
            pltpu.VMEM((4, C, C), F32),
            pltpu.VMEM((N, N), F32),
            pltpu.SemaphoreType.DMA((SEMS,)),
            pltpu.SemaphoreType.DMA((SEMS,)),
            pltpu.SemaphoreType.DMA((8,)),
        ],
        compiler_params=pltpu.CompilerParams(
            collective_id=0, has_side_effects=True, vmem_limit_bytes=56 * MIB
        ),
        cost_estimate=pl.CostEstimate(
            flops=8 * cells * C, bytes_accessed=4 * cells, transcendentals=2 * cells
        ),
        name="triangle_updates",
    )(pair, mask, in_gain, in_bias, proj, gate_w, out_gain, out_bias, out_w)


def solution(mesh):
    placed = (P("row", "col", None), P("row", "col"), P(), P(), P(), P(), P(), P(), P())
    return jax.shard_map(
        per_device, mesh=mesh, in_specs=placed, out_specs=P("row", "col", None), check_vma=False
    )
```

time: 364 us -> 174 us (0.48); the launches traced: 358 us -> 172 us
  waiting for transfers between devices: 186 us -> 0 us
  Pallas kernels: 0 us -> 168 us
  local copies, waits for them, and re-layouts: 58.1 us -> 4.79 us
  matrix products: 49.1 us -> 0 us
  other arithmetic: 36.8 us -> 0 us
  starting transfers between devices: 14.5 us -> 0 us
  between operations: 13.6 us -> 0.01 us
    all_gather x4 -> x0, waiting for transfers between devices: 175 us -> none  [the longest x1 70.7 us: per_device(): right_side = lax.all_gather(swapped, 'row', axis=1, tiled=True)]
    pallas_call x0 -> x1, Pallas kernels: none -> 168 us  [per_device(): pl.pallas_call(kernel, out_shape=jax.ShapeDtypeStruct((N, N, C), BF16), i...]
    dot_general x8 -> x0, matrix products: 49.1 us -> none  [the longest x2 19.8 us: finish(): jnp.dot(scaled.reshape(-1, channels), out_w, preferred_element_type=jnp.f...]
    convert_element_type x4 -> x0, local copies, waits for them, and re-layouts: 27.6 us -> none  [the longest x2 14.5 us: finish(): scaled = normalize(summed, gain_out, bias_out).astype(jnp.bfloat16)]
    all_gather x4 -> x0, local copies, waits for them, and re-layouts: 26.9 us -> none  [the longest x1 6.75 us: per_device(): left_side = lax.all_gather(swapped, 'col', axis=0, tiled=True)]
    reduce_sum x5 -> x0, other arithmetic: 18.5 us -> none  [the longest x4 12.8 us: normalize(): variance = jnp.mean(shifted * shifted, -1, keepdims=True)]
    convert_element_type x8 -> x0, other arithmetic: 18.2 us -> none  [the longest x1 7.48 us: per_device(): normalize(pair.astype(jnp.float32), in_gain[0], in_bias[0])]
    ppermute x2 -> x0, starting transfers between devices: 13.9 us -> none  [swap_axes(): return lax.ppermute(value, ('row', 'col'), pairs)]
  transfers between devices with their start and end apart: 6 -> 0, of which waited for: 6 -> 0; matrix products, arithmetic and copies ran while one was open for 13% -> 0% of each run, Pallas kernels for 0% -> 0%
where the time goes in v2:
time: 174 us; the launch traced here: 172 us
  Pallas kernels  168 us (97%)
  local copies, waits for them, and re-layouts  4.79 us (3%)
    pallas_call x1, Pallas kernels, per_device(): pl.pallas_call(kernel, out_shape=jax.ShapeDtypeStruct((N, N, C), BF16), i...  168 us
    unnamed x1, local copies, waits for them, and re-layouts  4.79 us

profile of v2, /device:TPU:1, one launch (start us, length us, event | category | flops | bytes accessed | tf_op | source)
XLA Modules:
  0.0 172.4 jit_solution(1598762730415345634)
XLA Ops:
  0.0 167.6 %triangle_updates.1 = bf16[128,128,128]{2,1,0:T(8,128)(2,1)} custom-call(bf16[128,128,128]{2,1,0:T(8,128)(2,1)} %pair_ref.1, s32[128,128]{1,0:T(8,128)} %mask_ref.1, f32[2,128]{1,0:T(2,128)} %ing_ref.1, f32[2,128]{1,0:T(2,128)} %inb_ref.1, bf16[2,128,512]{2,1,0:T(8,128)(2,1)} %pw_ref.1, bf16[2,128,128]{2,1,0:T(8,128)(2,1)} %gw_ref.1, f32[2,128]{1,0:T(2,128)} %outg_ref.1, ...), custom_call_target="tpu_custom_call" | custom-call | flops 2147483648 | bytes 8388608 | tf_op jit(solution)/shard_map/triangle_updates/pallas_call | solution.py:387
  167.6 4.8 %copy.11 = bf16[128,128,128]{2,1,0:T(8,128)(2,1)} copy(bf16[128,128,128]{2,1,0:T(8,128)(2,1)} %triangle_updates.1) | data formatting | bytes 8388608

commit v3 on v2

--- a/solution.py
+++ b/solution.py
@@ -14,6 +14,8 @@
 PIECE = C * WIN
 HALF = PIECE // 2
 EPS = 1e-5
+GATE = 4
+UNROLL = 4
 MIB = 1024 * 1024
 SEMS = 160
 F32 = jnp.float32
@@ -27,6 +29,11 @@
     return total
 
 
+def flip(a):
+    low, next_ = lax.rem(a, 2), lax.rem(lax.div(a, 2), 2)
+    return a - low - 2 * next_ + 2 * low + next_
+
+
 def sigmoid(z):
     return 0.5 * jnp.tanh(0.5 * z) + 0.5
 
@@ -40,14 +47,17 @@
 
 def kernel(
     pair_ref, mask_ref, ing_ref, inb_ref, pw_ref, gw_ref, outg_ref, outb_ref, ow_ref, out_ref,
-    wbuf, pairv, gate, a1, b1, a2, b2, xs, ha, hb, hat, hbt, own, mid_sw, parity, cols, maskt,
+    wbuf, pairv, gate, a1, b1, a2, b2, xs, ha, hb, hat, hbt, own, mid_sw, parity, mean_w, cols, maskt,
     ssem, rsem, lsem,
 ):
     r = lax.axis_index("row")
     c = lax.axis_index("col")
     y, zh = lax.div(r, 4), lax.rem(r, 4)
     zl, x, core = lax.div(c, 8), lax.rem(lax.div(c, 2), 4), lax.rem(c, 2)
-    rc = xor(r, c)
+    via_row = xor(r, flip(c))
+    via_col = flip(xor(r, c))
+
+    to_col = xor(r, flip(c))
 
     def row_at(dz, dy):
         return lax.rem(y + dy + 4, 4) * 4 + lax.rem(zh + dz + 4, 4)
@@ -76,11 +86,12 @@
 
     @pl.when(c != 0)
     def _():
-        greet((rc, c))
-
-    @pl.when(r != 0)
+        greet((via_row, c))
+
+    @pl.when(to_col != c)
     def _():
-        greet((r, rc))
+        greet((r, to_col))
+        greet((r, via_col))
 
     copies = {}
 
@@ -107,6 +118,7 @@
         low = lax.rem(row, 16) < 8
         parity[0] = jnp.where(low, 1.0, 0.0).astype(BF16)
         parity[1] = jnp.where(low, 0.0, 1.0).astype(BF16)
+        mean_w[...] = jnp.full((C, C), 1.0 / C, BF16)
         for d in range(2):
             cols[2 * d] = jnp.broadcast_to(outg_ref[pl.ds(d, 1), :], (C, C)).T
             cols[2 * d + 1] = jnp.broadcast_to(outb_ref[pl.ds(d, 1), :], (C, C)).T
@@ -152,16 +164,18 @@
         g, b = ing_ref[pl.ds(d, 1), :], inb_ref[pl.ds(d, 1), :]
 
         def body(t, carry):
-            v = pairv[pl.ds(t * 2, 2)].astype(F32).reshape(2 * N, C)
-            n = norm_lanes(v, g, b).astype(BF16)
+            v = pairv[pl.ds(t * GATE, GATE)].reshape(GATE * N, C)
+            s = v.astype(F32) - jnp.dot(v, mean_w[...], preferred_element_type=F32)
+            var = jnp.dot((s * s).astype(BF16), mean_w[...], preferred_element_type=F32)
+            n = (s * lax.rsqrt(var + EPS) * g + b).astype(BF16)
             z = jnp.dot(n, gw_ref[d], preferred_element_type=F32)
-            gate[pl.ds(t * 2, 2)] = sigmoid(z).astype(BF16).reshape(2, N, C)
+            gate[pl.ds(t * GATE, GATE)] = sigmoid(z).astype(BF16).reshape(GATE, N, C)
             return carry
 
-        lax.fori_loop(lo // 2, hi // 2, body, 0)
+        lax.fori_loop(lo // GATE, hi // GATE, body, 0)
 
     def product(a, b, lo, hi):
-        def body(t, carry):
+        def one(t):
             rows = pl.ds(pl.multiple_of(t * 16, 16), 16)
             lhs = a[:, rows, :].reshape(256, N)
             rhs = b[:, rows, :].reshape(256, N)
@@ -170,9 +184,13 @@
             base = pl.multiple_of(t * 16, 16)
             xs[:, pl.ds(base, 8), :] = out[:, :N].reshape(16, 8, N)
             xs[:, pl.ds(base + 8, 8), :] = out[:, N:].reshape(16, 8, N)
+
+        def body(t, carry):
+            for k in range(UNROLL):
+                one(t * UNROLL + k)
             return carry
 
-        lax.fori_loop(lo, hi, body, 0)
+        lax.fori_loop(lo // UNROLL, hi // UNROLL, body, 0)
 
     def finish(lo, hi, d):
         def body(t, carry):
@@ -195,10 +213,13 @@
     def gather_steps(p, a, b, lab_a, lab_b):
         steps = []
 
-        def b_first(h):
+        def b_first_z(h):
             s = half(b, lab_b(r), h)
             for dz in (1, -1):
                 post((p, "z", dz, h), s, s, (row_at(dz, 0), c))
+
+        def b_first_y(h):
+            s = half(b, lab_b(r), h)
             for dy in (1, -1):
                 post((p, "y", 0, dy, h), s, s, (row_at(0, dy), c))
 
@@ -258,11 +279,18 @@
                         got((p, "k", q, dx, h))
 
         f = functools.partial
-        bs = [f(b_z, 1, 0), f(b_z, -1, 0), f(b_z, 1, 1), f(b_z, -1, 1), f(b_z2, 0), f(b_z2, 1)]
-        for q in (0, 1, -1, 2):
-            for h in (0, 1):
+        zs = [f(b_z, 1, 0), f(b_z, -1, 0), f(b_z, 1, 1), f(b_z, -1, 1)]
+        bs = []
+        for h in (0, 1):
+            bs += [f(b_y, 0, 1, h), f(b_y, 0, -1, h)]
+        bs += [f(b_z2, 0), f(b_z2, 1)]
+        for h in (0, 1):
+            for q in (1, -1):
                 bs += [f(b_y, q, 1, h), f(b_y, q, -1, h)]
-        for q in (0, 1, -1, 2):
+        bs += [f(b_y2, 0, 0), f(b_y2, 0, 1)]
+        for h in (0, 1):
+            bs += [f(b_y, 2, 1, h), f(b_y, 2, -1, h)]
+        for q in (1, -1, 2):
             bs += [f(b_y2, q, 0), f(b_y2, q, 1)]
         as_ = [f(a_l, 0), f(a_l, 1)]
         for q in (0, 1):
@@ -271,12 +299,14 @@
         for q in (0, 1):
             as_ += [f(a_x2, q, 0), f(a_x2, q, 1)]
         as_ += [a_k]
-        return b_first, bs, a_first, as_
-
-    def weave(*lists):
+        return b_first_z, b_first_y, zs, bs, a_first, as_
+
+    def weave(*lists, late=(0.0, 0.0, 0.0)):
         keyed = []
         for n, items in enumerate(lists):
-            keyed += [((k + 0.5) / len(items), n, k, item) for k, item in enumerate(items)]
+            for k, item in enumerate(items):
+                at = late[n] + (1.0 - late[n]) * (k + 0.5) / len(items)
+                keyed.append((at, n, k, item))
         return [e[3] for e in sorted(keyed, key=lambda e: e[:3])]
 
     def swap(name, src, dst, dev, moves):
@@ -307,28 +337,37 @@
     window_out()
     a1[c] = hat[...].astype(BF16)
     own[0] = hbt[...].astype(BF16)
-    pl.semaphore_wait(bar, 8 + jnp.where(c != 0, 1, 0) + jnp.where(r != 0, 1, 0))
-    for h in (0, 1):
-        swap(("s1", h), part(own.at[0], h), part(mid_sw.at[0], h), (rc, c), c != 0)
-    b_first, bs, a_first, as_ = gather_steps(0, a1, b1, lambda col: col, lambda row: xor(row, c))
-    a_first(0)
-    a_first(1)
-    load_p.wait()
+    pl.semaphore_wait(bar, 8 + jnp.where(c != 0, 1, 0) + jnp.where(to_col != c, 2, 0))
+    def swap1(h):
+        swap(("s1", h), part(own.at[0], h), part(mid_sw.at[0], h), (via_row, c), c != 0)
 
     def relay1(h):
         swapped(("s1", h), c != 0)
-        swap(("s2", h), part(mid_sw.at[0], h), half(b1, c, h), (r, rc), r != 0)
-
-    def begin1(h):
-        swapped(("s2", h), r != 0)
-        b_first(h)
-
+        swap(("s2", h), part(mid_sw.at[0], h), half(b1, c, h), (r, to_col), to_col != c)
+
+    swap1(0)
+    bz, by, zs, bs, a_first, as_ = gather_steps(
+        0, a1, b1, lambda col: col, lambda row: flip(xor(row, c))
+    )
+    load_p.wait()
     gates = [f(gate_rows, 8 * t, 8 * t + 8, 0) for t in range(16)]
-    for step in weave([f(relay1, 0), f(relay1, 1)], gates[:3]):
-        step()
-    for step in weave([f(begin1, 0), f(begin1, 1)], as_[:4], gates[3:7]):
-        step()
-    for step in weave(bs, as_[4:], gates[7:]):
+    gates[0]()
+    relay1(0)
+    swap1(1)
+    gates[1]()
+    relay1(1)
+    swapped(("s2", 0), to_col != c)
+    bz(0)
+    by(0)
+    a_first(0)
+    gates[2]()
+    swapped(("s2", 1), to_col != c)
+    by(1)
+    zs[0]()
+    zs[1]()
+    bz(1)
+    a_first(1)
+    for step in weave(bs[:2] + zs[2:] + bs[2:], as_, gates[3:], late=(0.0, 0.2, 0.0)):
         step()
 
     product(a1, b1, 0, 64)
@@ -336,30 +375,41 @@
     window_in()
     own[1] = hat[...].astype(BF16)
     b2[r] = hbt[...].astype(BF16)
-    b_first, bs, a_first, as_ = gather_steps(1, a2, b2, lambda col: xor(r, col), lambda row: row)
-    for h in (0, 1):
-        swap(("t1", h), part(own.at[1], h), part(mid_sw.at[1], h), (r, rc), r != 0)
-    b_first(0)
-    b_first(1)
+    bz, by, zs, bs, a_first, as_ = gather_steps(
+        1, a2, b2, lambda col: xor(r, flip(col)), lambda row: row
+    )
+
+    def swap2(h):
+        swap(("t1", h), part(own.at[1], h), part(mid_sw.at[1], h), (r, via_col), to_col != c)
 
     def relay2(h):
-        swapped(("t1", h), r != 0)
-        swap(("t2", h), part(mid_sw.at[1], h), half(a2, r, h), (rc, c), c != 0)
+        swapped(("t1", h), to_col != c)
+        swap(("t2", h), part(mid_sw.at[1], h), half(a2, r, h), (via_row, c), c != 0)
 
     def begin2(h):
         swapped(("t2", h), c != 0)
         a_first(h)
 
-    rest = []
-    for t in range(1, 16):
-        rest.append(f(finish, t, t + 1, 0))
-    gates = [f(gate_rows, 8 * t, 8 * t + 8, 1) for t in range(16)]
-    work = rest + gates
-    for step in weave([f(relay2, 0), f(relay2, 1)], work[:4]):
+    swap2(0)
+    bz(0)
+    by(0)
+    by(1)
+    work = [f(finish, t, t + 1, 0) for t in range(1, 16)]
+    work += [f(gate_rows, 8 * t, 8 * t + 8, 1) for t in range(16)]
+    for step in work[:5]:
         step()
-    for step in weave([f(begin2, 0), f(begin2, 1)], bs[:2], work[4:8]):
+    relay2(0)
+    swap2(1)
+    zs[0]()
+    zs[1]()
+    bz(1)
+    for step in work[5:8]:
         step()
-    for step in weave(bs[2:], as_, work[8:]):
+    relay2(1)
+    begin2(0)
+    for step in bs[:2] + work[8:10] + zs[2:] + bs[2:4] + [f(begin2, 1)]:
+        step()
+    for step in weave(bs[4:], as_, work[10:]):
         step()
 
     product(a2, b2, 0, 64)
@@ -370,7 +420,7 @@
         cp = pltpu.make_async_copy(pairv.at[rows], out_ref.at[rows], lsem.at[3 + t])
         cp.start()
         outs.append(cp)
-    guard = {"s1": c != 0, "s2": r != 0, "t1": r != 0, "t2": c != 0}
+    guard = {"s1": c != 0, "s2": to_col != c, "t1": to_col != c, "t2": c != 0}
     for name, cp in copies.items():
         if name[0] in guard:
             pl.when(guard[name[0]])(cp.wait_send)
@@ -405,6 +455,7 @@
             pltpu.VMEM((2, PIECE, N), BF16),
             pltpu.VMEM((2, PIECE, N), BF16),
             pltpu.VMEM((2, 256, N), BF16),
+            pltpu.VMEM((C, C), BF16),
             pltpu.VMEM((4, C, C), F32),
             pltpu.VMEM((N, N), F32),
             pltpu.SemaphoreType.DMA((SEMS,)),

time: 174 us -> 149 us (0.86)
  Pallas kernels: 168 us -> 142 us
    pallas_call x1, Pallas kernels: 168 us -> 142 us  [per_device(): pl.pallas_call(kernel, out_shape=jax.ShapeDtypeStruct((N, N, C), BF16), i...]
where the time goes in v3:
time: 149 us; the launch traced here: 147 us
  Pallas kernels  142 us (95%)
  local copies, waits for them, and re-layouts  4.79 us (3%)
    pallas_call x1, Pallas kernels, per_device(): pl.pallas_call(kernel, out_shape=jax.ShapeDtypeStruct((N, N, C), BF16), i...  142 us
    unnamed x1, local copies, waits for them, and re-layouts  4.79 us

profile of v3, /device:TPU:1, one launch (start us, length us, event | category | flops | bytes accessed | tf_op | source)
XLA Modules:
  0.0 146.6 jit_solution(9485530750928991516)
XLA Ops:
  0.0 141.8 %triangle_updates.1 = bf16[128,128,128]{2,1,0:T(8,128)(2,1)} custom-call(bf16[128,128,128]{2,1,0:T(8,128)(2,1)} %pair_ref.1, s32[128,128]{1,0:T(8,128)} %mask_ref.1, f32[2,128]{1,0:T(2,128)} %ing_ref.1, f32[2,128]{1,0:T(2,128)} %inb_ref.1, bf16[2,128,512]{2,1,0:T(8,128)(2,1)} %pw_ref.1, bf16[2,128,128]{2,1,0:T(8,128)(2,1)} %gw_ref.1, f32[2,128]{1,0:T(2,128)} %outg_ref.1, ...), custom_call_target="tpu_custom_call" | custom-call | flops 2147483648 | bytes 8388608 | tf_op jit(solution)/shard_map/triangle_updates/pallas_call | solution.py:437
  141.8 4.8 %copy.11 = bf16[128,128,128]{2,1,0:T(8,128)(2,1)} copy(bf16[128,128,128]{2,1,0:T(8,128)(2,1)} %triangle_updates.1) | data formatting | bytes 8388608

commit v4 on v3

--- a/solution.py
+++ b/solution.py
@@ -15,7 +15,7 @@
 HALF = PIECE // 2
 EPS = 1e-5
 GATE = 4
-UNROLL = 4
+UNROLL = 8
 MIB = 1024 * 1024
 SEMS = 160
 F32 = jnp.float32

time: 149 us -> 146 us (0.980)
  Pallas kernels: 142 us -> 138 us
    pallas_call x1, Pallas kernels: 142 us -> 138 us  [per_device(): pl.pallas_call(kernel, out_shape=jax.ShapeDtypeStruct((N, N, C), BF16), i...]
where the time goes in v4:
time: 146 us; the launch traced here: 143 us
  Pallas kernels  138 us (95%)
  local copies, waits for them, and re-layouts  4.79 us (3%)
    pallas_call x1, Pallas kernels, per_device(): pl.pallas_call(kernel, out_shape=jax.ShapeDtypeStruct((N, N, C), BF16), i...  138 us
    unnamed x1, local copies, waits for them, and re-layouts  4.79 us

profile of v4, /device:TPU:1, one launch (start us, length us, event | category | flops | bytes accessed | tf_op | source)
XLA Modules:
  0.0 143.2 jit_solution(4170782858768943389)
XLA Ops:
  0.0 138.4 %triangle_updates.1 = bf16[128,128,128]{2,1,0:T(8,128)(2,1)} custom-call(bf16[128,128,128]{2,1,0:T(8,128)(2,1)} %pair_ref.1, s32[128,128]{1,0:T(8,128)} %mask_ref.1, f32[2,128]{1,0:T(2,128)} %ing_ref.1, f32[2,128]{1,0:T(2,128)} %inb_ref.1, bf16[2,128,512]{2,1,0:T(8,128)(2,1)} %pw_ref.1, bf16[2,128,128]{2,1,0:T(8,128)(2,1)} %gw_ref.1, f32[2,128]{1,0:T(2,128)} %outg_ref.1, ...), custom_call_target="tpu_custom_call" | custom-call | flops 2147483648 | bytes 8388608 | tf_op jit(solution)/shard_map/triangle_updates/pallas_call | solution.py:437
  138.4 4.8 %copy.11 = bf16[128,128,128]{2,1,0:T(8,128)(2,1)} copy(bf16[128,128,128]{2,1,0:T(8,128)(2,1)} %triangle_updates.1) | data formatting | bytes 8388608
